TPU v7x, 256 devices: a whole 4x4x8 slice. The times are simulated.
256 devices in a mesh: blk: 8 (over y, core), req: 32 (over z, x).
Axes of the slice: x: 4, y: 4, z: 8, core: 2. Of those that a mesh axis runs over, the one named last changes fastest.
Arguments:
- hidden: bfloat16 [12288, 8192], P('req', 'blk'), may hold values from -120 to 120
- input_norm_gain: float32 [8192], replicated, may hold values from 0.1 to 1.9
- query_weight: bfloat16 [8192, 8192], P('req', 'blk')
- keyvalue_weight: bfloat16 [8192, 2048], P('req', 'blk')
- adapter_down: bfloat16 [32, 3, 16, 8192], P('req', None, None, 'blk'), may hold values from -0.0625 to 0.0625
- adapter_up_query: bfloat16 [32, 16, 8192], P('req', None, 'blk'), may hold values from -1.5 to 1.5
- adapter_up_keyvalue: bfloat16 [32, 16, 2048], P('req', None, 'blk'), may hold values from -1.5 to 1.5
- packed_lengths: int32 [32, 4], P('req'), may hold values from 1 to 192, 384 in all within a row
- prompt_adapter: int32 [32, 4], P('req'), may hold values from 0 to 31
Outputs:
- context: bfloat16 [12288, 8192], P('req', 'blk')
- key_cache: bfloat16 [12288, 1024], P('req', 'blk')
- value_cache: bfloat16 [12288, 1024], P('req', 'blk')
Inputs may be any that keep to these rules, and one draw needn't show every extreme that they name: `packed_lengths`: each row sums to 384; the longest prompt of the whole draw has 192 tokens.
All inputs are finite; a program needn't handle non-finite values.
Results may differ from a plain program's by a relative error of at most 0.012.
The roundings to bfloat16 on the way count: a program that leaves them out, or rounds other values in their place, can miss the bound.
Values may be sent and summed in bfloat16 or wider, within the bound.
A program may use at most 128 MiB of HBM per device.

v0:
```python
import math
import jax
import jax.numpy as jnp
from jax import lax
from jax.sharding import PartitionSpec as P

HEAD_WIDTH = 128
QUERY_LOCAL = 8
KEYVALUE_LOCAL = 1
epsilon = 1e-05
adapter_scale = 2.0
rope_base = 10000.0


def apply_rotation(vectors, cosine_table, sine_table):
    half_size = vectors.shape[-1] // 2
    first_half = vectors[..., :half_size]
    second_half = vectors[..., half_size:]
    turned = jnp.concatenate([-second_half, first_half], axis=-1)
    return vectors * cosine_table + turned * sine_table


def layout(lengths, count):
    slot_index = jnp.arange(count, dtype=jnp.int32)
    prompt_ends = jnp.cumsum(lengths)
    prompt_starts = prompt_ends - lengths
    member = (slot_index[:, None] >= prompt_starts[None, :]) & (
        slot_index[:, None] < prompt_ends[None, :]
    )
    position = jnp.sum(jnp.where(member, slot_index[:, None] - prompt_starts[None, :], 0), axis=1)
    owner = jnp.sum((slot_index[:, None] >= prompt_ends[None, :]).astype(jnp.int32), axis=1)
    return (member.astype(jnp.float32), position, owner, slot_index)


def rope_tables(position, head_size):
    frequency = rope_base ** (-(jnp.arange(head_size // 2, dtype=jnp.float32) * 2.0 / head_size))
    angles = position.astype(jnp.float32)[:, None] * frequency[None, :]
    cosine_table = jnp.cos(angles)
    sine_table = jnp.sin(angles)
    return (
        jnp.concatenate([cosine_table, cosine_table], 1)[:, None, :],
        jnp.concatenate([sine_table, sine_table], 1)[:, None, :],
    )


def shards(
    hidden,
    input_norm_gain,
    query_weight,
    keyvalue_weight,
    adapter_down,
    adapter_up_query,
    adapter_up_keyvalue,
    packed_lengths,
    prompt_adapter,
):
    row_number, feature_cols = hidden.shape
    full_width = feature_cols * lax.axis_size("blk")
    offset = lax.axis_index("blk") * feature_cols
    values = hidden.astype(jnp.float32)
    gain_part = lax.dynamic_slice_in_dim(input_norm_gain, offset, feature_cols, 0)
    squares = lax.psum(jnp.sum(values * values, axis=1), "blk")
    factor = lax.rsqrt(squares / full_width + epsilon)
    normed_part = (values * factor[:, None] * gain_part[None, :]).astype(jnp.bfloat16)
    normed = lax.all_gather(normed_part, "blk", axis=1, tiled=True)
    query_cols = query_weight.shape[1]

    def add_rows(weight_piece):
        return jnp.dot(normed, weight_piece, preferred_element_type=jnp.float32)

    query_plain = add_rows(lax.all_gather(query_weight, "req", axis=0, tiled=True))
    base_pair = add_rows(lax.all_gather(keyvalue_weight, "req", axis=0, tiled=True))
    down_all, up_query_all, up_pair_all = (
        lax.all_gather(adapter_down, "req", axis=0, tiled=True),
        lax.all_gather(adapter_up_query, "req", axis=0, tiled=True),
        lax.all_gather(adapter_up_keyvalue, "req", axis=0, tiled=True),
    )
    adapter_count = down_all.shape[0]
    lengths = packed_lengths[0]
    member, position, owner, slot_index = layout(lengths, row_number)
    prompt_count = lengths.shape[0]
    picked_adapter = (
        prompt_adapter[0][:, None] == jnp.arange(adapter_count, dtype=jnp.int32)[None, :]
    ).astype(jnp.bfloat16)
    down_selected = jnp.einsum(
        "pa,ajrd->pjrd", picked_adapter, down_all, preferred_element_type=jnp.float32
    ).astype(jnp.bfloat16)
    rank_size = down_selected.shape[2]
    partial_value = lax.dot_general(
        normed_part,
        down_selected.reshape(prompt_count * 3 * rank_size, feature_cols),
        (((1,), (1,)), ((), ())),
        preferred_element_type=jnp.float32,
    )
    partial_value = partial_value.reshape(row_number, prompt_count, 3, rank_size)
    masked = jnp.sum(partial_value * member[:, :, None, None], axis=1).reshape(
        row_number, 3 * rank_size
    )
    low_rank = lax.psum(masked, "blk").reshape(row_number, 3, rank_size).astype(jnp.bfloat16)
    low_float = low_rank.astype(jnp.float32)

    def spread(column):
        return (
            (member[:, :, None] * low_float[:, None, column, :])
            .astype(jnp.bfloat16)
            .reshape(row_number, prompt_count * rank_size)
        )

    up_query_selected = jnp.einsum(
        "pa,arc->prc", picked_adapter, up_query_all, preferred_element_type=jnp.float32
    ).astype(jnp.bfloat16)
    up_keyvalue_selected = jnp.einsum(
        "pa,arc->prc", picked_adapter, up_pair_all, preferred_element_type=jnp.float32
    ).astype(jnp.bfloat16)
    up_keyvalue_selected = up_keyvalue_selected.reshape(
        prompt_count, rank_size, KEYVALUE_LOCAL, 2, HEAD_WIDTH
    )
    query_update = jnp.dot(
        spread(0),
        up_query_selected.reshape(prompt_count * rank_size, query_cols),
        preferred_element_type=jnp.float32,
    )
    key_update = jnp.dot(
        spread(1),
        up_keyvalue_selected[:, :, :, 0].reshape(
            prompt_count * rank_size, KEYVALUE_LOCAL * HEAD_WIDTH
        ),
        preferred_element_type=jnp.float32,
    )
    value_update = jnp.dot(
        spread(2),
        up_keyvalue_selected[:, :, :, 1].reshape(
            prompt_count * rank_size, KEYVALUE_LOCAL * HEAD_WIDTH
        ),
        preferred_element_type=jnp.float32,
    )
    cosine_table, sine_table = rope_tables(position, HEAD_WIDTH)
    query_complete = (query_plain + adapter_scale * query_update).reshape(
        row_number, QUERY_LOCAL * KEYVALUE_LOCAL, HEAD_WIDTH
    )
    query_states = apply_rotation(query_complete, cosine_table, sine_table).astype(jnp.bfloat16)
    keyvalue_plain = base_pair.reshape(row_number, KEYVALUE_LOCAL, 2, HEAD_WIDTH)
    key_vectors = apply_rotation(
        keyvalue_plain[:, :, 0]
        + adapter_scale * key_update.reshape(row_number, KEYVALUE_LOCAL, HEAD_WIDTH),
        cosine_table,
        sine_table,
    ).astype(jnp.bfloat16)
    value_vectors = (
        keyvalue_plain[:, :, 1]
        + adapter_scale * value_update.reshape(row_number, KEYVALUE_LOCAL, HEAD_WIDTH)
    ).astype(jnp.bfloat16)
    grouped = query_states.reshape(row_number, KEYVALUE_LOCAL, QUERY_LOCAL, HEAD_WIDTH)
    scores = jnp.einsum(
        "tkgc,skc->kgts", grouped, key_vectors, preferred_element_type=jnp.float32
    ) / math.sqrt(HEAD_WIDTH)
    allowed = (owner[:, None] == owner[None, :]) & (slot_index[None, :] <= slot_index[:, None])
    scores = jnp.where(allowed[None, None], scores, -1e30)
    row_max = jnp.max(scores, axis=-1, keepdims=True)
    exponent = jnp.exp(scores - row_max)
    attend = (exponent / jnp.sum(exponent, axis=-1, keepdims=True)).astype(jnp.bfloat16)
    context = jnp.einsum(
        "kgts,skc->tkgc", attend, value_vectors, preferred_element_type=jnp.float32
    ).astype(jnp.bfloat16)
    return (
        context.reshape(row_number, KEYVALUE_LOCAL * QUERY_LOCAL * HEAD_WIDTH),
        key_vectors.reshape(row_number, KEYVALUE_LOCAL * HEAD_WIDTH),
        value_vectors.reshape(row_number, KEYVALUE_LOCAL * HEAD_WIDTH),
    )


def solution(mesh):
    in_specs = (
        P("req", "blk"),
        P(),
        P("req", "blk"),
        P("req", "blk"),
        P("req", None, None, "blk"),
        P("req", None, "blk"),
        P("req", None, "blk"),
        P("req", None),
        P("req", None),
    )
    out_specs = (P("req", "blk"), P("req", "blk"), P("req", "blk"))
    return jax.shard_map(shards, mesh=mesh, in_specs=in_specs, out_specs=out_specs, check_vma=False)
```

profile of v0, /device:TPU:1, one launch (start us, length us, event | category | flops | bytes accessed | tf_op | source)
XLA Modules:
  0.0 463.0 jit_solution(1548275453089813098)
XLA Ops:
  7.2 0.7 all-gather.14.cloned.1.call-update
  8.0 0.7 all-gather.10.cloned.1.call-update
  8.7 0.7 all-gather.8.cloned.1.call-update
  9.4 0.7 dynamic_slice.3
  10.1 1.4 fusion.7
  11.5 15.0 %psum.14 = f32[384]{0:T(512)S(1)} all-reduce(f32[384]{0:T(512)S(1)} %fusion.7), channel_id=1, replica_groups=mesh['blk'=8,'req'=32] {'blk'}, use_global_device_ids=true, to_apply=%region_1.0 | all-reduce | flops 384 | bytes 3072 | tf_op jit(solution)/shard_map/psum | solution.py:62
  26.6 1.1 fusion.9
  28.5 40.4 %all_gather.21 = bf16[32,16,256]{2,1,0:T(8,128)(2,1)S(1)} all-gather(bf16[1,16,256]{2,1,0:T(8,128)(2,1)S(1)} %copy-done.4), channel_id=1, replica_groups=mesh['blk'=8,'req'=32] {'req'}, dimensions={0}, use_global_device_ids=true | all-gather | bytes 270336 | tf_op jit(solution)/shard_map/all_gather | solution.py:76
  69.6 0.8 multiply_cosine_fusion
  70.4 16.0 %all-gather.14.cloned.1.call-done = bf16[32,16,1024]{2,1,0:T(8,128)(2,1)} async-done(((bf16[1,16,1024]{2,1,0:T(8,128)(2,1)}), bf16[32,16,1024]{2,1,0:T(8,128)(2,1)}) %all-gather.14.cloned.1.call-update) | async-done | bytes 1048592 | tf_op jit(solution)/shard_map/all_gather | solution.py:75
  86.3 2.4 convolution_convert_fusion
  88.8 78.0 %all-gather.10.cloned.1.call-done = bf16[32,3,16,1024]{3,2,1,0:T(8,128)(2,1)} async-done(((bf16[1,3,16,1024]{3,2,1,0:T(8,128)(2,1)}), bf16[32,3,16,1024]{3,2,1,0:T(8,128)(2,1)}) %all-gather.10.cloned.1.call-update) | async-done | bytes 3145744 | tf_op jit(solution)/shard_map/all_gather | solution.py:74
  166.8 5.4 %fusion.15 = bf16[4,3,16,1024]{3,0,2,1:T(4,128)(2,1)S(1)} fusion(bf16[32,3,16,1024]{3,2,1,0:T(8,128)(2,1)} %all-gather.10.cloned.1.call-done, s32[4]{0:T(128)S(1)} %bitcast.137), kind=kOutput, calls=%fused_computation.23 | convolution fusion | flops 12779648 | bytes 3538960 | tf_op jit(solution)/shard_map/pa,ajrd->pjrd/dot_general | solution.py:85
  172.6 26.5 %psum.15 = bf16[384,48]{0,1:T(8,128)(2,1)S(1)} all-reduce(f32[384,48]{0,1:T(8,128)S(1)} %bitcast.132), channel_id=1, replica_groups=mesh['blk'=8,'req'=32] {'blk'}, use_global_device_ids=true, to_apply=%region_4.5 | all-reduce | flops 18432 | bytes 110592 | tf_op jit(solution)/shard_map/psum | solution.py:99
  199.5 49.6 %all-gather.8.cloned.1.call-done = bf16[8192,256]{1,0:T(8,128)(2,1)} async-done(((bf16[256,256]{1,0:T(8,128)(2,1)}), bf16[8192,256]{1,0:T(8,128)(2,1)}) %all-gather.8.cloned.1.call-update) | async-done | bytes 4194320 | tf_op jit(solution)/shard_map/all_gather | solution.py:72
  249.1 46.2 %all-gather.6.cloned.1.call-done = bf16[384,8192]{1,0:T(8,128)(2,1)} async-done(((bf16[384,1024]{1,0:T(8,128)(2,1)}), bf16[384,8192]{1,0:T(8,128)(2,1)}) %all-gather.6.cloned.1.call-update) | async-done | bytes 6291472 | tf_op jit(solution)/shard_map/all_gather | solution.py:65
  295.4 6.4 %fusion.55 = f32[384,256]{0,1:T(8,128)S(1)} fusion(bf16[384,8192]{1,0:T(8,128)(2,1)} %all-gather.6.cloned.1.call-done, bf16[8192,256]{1,0:T(8,128)(2,1)} %all-gather.8.cloned.1.call-done), kind=kOutput, calls=%fused_computation.86 | convolution fusion | flops 1610612736 | bytes 10878976 | tf_op jit(solution)/shard_map/dot_general | solution.py:69
  302.9 134.8 %all-gather.12.cloned.1.call-done = bf16[8192,1024]{1,0:T(8,128)(2,1)} async-done(((bf16[256,1024]{1,0:T(8,128)(2,1)}), bf16[8192,1024]{1,0:T(8,128)(2,1)}) %all-gather.12.cloned.1.call-update) | async-done | bytes 16777232 | tf_op jit(solution)/shard_map/all_gather | solution.py:71
  437.7 12.0 %fusion.11 = f32[384,1024]{1,0:T(8,128)S(1)} fusion(f32[384,1024,1]{1,0,2:T(8,128)S(1)} %fusion.34, bf16[384,8192]{1,0:T(8,128)(2,1)} %all-gather.6.cloned.1.call-done, bf16[8192,1024]{1,0:T(8,128)(2,1)} %all-gather.12.cloned.1.call-done), kind=kOutput, calls=%fused_computation.21 | convolution fusion | flops 6443237376 | bytes 26214400 | tf_op jit(solution)/shard_map/dot_general | solution.py:69
  450.6 0.6 maximum_multiply_fusion
  451.2 1.4 fusion.1
  452.7 1.0 fusion
  453.7 1.6 fusion.12
  455.3 1.2 copy.43
  (49 shorter events, 4.5 us)
Async XLA Ops:
  7.2 19.4 %copy-start = (bf16[384,1024]{1,0:T(8,128)(2,1)S(1)}, bf16[384,1024]{1,0:T(8,128)(2,1)}, u32[]{:S(2)}) copy-start(bf16[384,1024]{1,0:T(8,128)(2,1)} %param.9) | copy-start | bytes 2359300
  7.2 79.1 %all-gather.14.cloned.1.call-start = ((), (), s32[]{:S(2)}) async-start(), calls=%async_computation.4 | async-start | bytes 1081344 | tf_op jit(solution)/shard_map/all_gather | solution.py:75
  7.9 158.9 %all-gather.10.cloned.1.call-start = ((), (), s32[]{:S(2)}) async-start(), calls=%async_computation.2 | async-start | bytes 3244032 | tf_op jit(solution)/shard_map/all_gather | solution.py:74
  8.7 240.5 %all-gather.8.cloned.1.call-start = ((), (), s32[]{:S(2)}) async-start(), calls=%async_computation.1 | async-start | bytes 4325376 | tf_op jit(solution)/shard_map/all_gather | solution.py:72
  9.4 286.0 %all-gather.6.cloned.1.call-start = ((), (), s32[]{:S(2)}) async-start(), calls=%async_computation | async-start | bytes 7077888 | tf_op jit(solution)/shard_map/all_gather | solution.py:65
  11.5 16.8 %copy-start.6 = (s32[1,4]{1,0:T(1,128)S(1)}, s32[1,4]{1,0:T(1,128)}, u32[]{:S(2)}) copy-start(s32[1,4]{1,0:T(1,128)} %param.16) | copy-start | bytes 52
  11.5 17.0 %copy-start.4 = (bf16[1,16,256]{2,1,0:T(8,128)(2,1)S(1)}, bf16[1,16,256]{2,1,0:T(8,128)(2,1)}, u32[]{:S(2)}) copy-start(bf16[1,16,256]{2,1,0:T(8,128)(2,1)} %param.15) | copy-start | bytes 24580
  26.5 42.4 %copy-start.5 = (s32[1,4]{1,0:T(1,128)S(1)}, s32[1,4]{1,0:T(1,128)}, u32[]{:S(2)}) copy-start(s32[1,4]{1,0:T(1,128)} %param.17) | copy-start | bytes 52
  27.7 410.0 %all-gather.12.cloned.1.call-start = ((), (), s32[]{:S(2)}) async-start(), calls=%async_computation.3 | async-start | bytes 17301504 | tf_op jit(solution)/shard_map/all_gather | solution.py:71
  88.8 83.4 %copy-start.1 = (bf16[384,1024]{1,0:T(8,128)(2,1)S(1)}, bf16[384,1024]{1,0:T(8,128)(2,1)}, u32[]{:S(2)}) copy-start(bf16[384,1024]{1,0:T(8,128)(2,1)} %fusion.9) | copy-start | bytes 2359300
  302.3 151.4 %copy-start.3 = (bf16[384,128]{1,0:T(8,128)(2,1)}, bf16[384,128]{1,0:T(8,128)(2,1)S(1)}, u32[]{:S(2)}) copy-start(bf16[384,128]{1,0:T(8,128)(2,1)S(1)} %fusion.21) | copy-start | bytes 294916
  302.9 148.4 %copy-start.2 = (bf16[384,128]{1,0:T(8,128)(2,1)}, bf16[384,128]{1,0:T(8,128)(2,1)S(1)}, u32[]{:S(2)}) copy-start(bf16[384,128]{1,0:T(8,128)(2,1)S(1)} %get-tuple-element.18) | copy-start | bytes 294916
Sparse Core Ops, SparseCore 0:
  10.6 75.6 all-gather.13
  88.9 77.8 all-gather.9
  169.3 79.7 all-gather.7
  251.4 43.9 all-gather.5
  297.8 139.8 all-gather.11
where the time goes:
time: 463 us
  waiting for transfers between devices  327 us (71%)
  blocking collectives  81.9 us (18%)
  matrix products  30.7 us (7%)
  between operations  14 us (3%)
  other arithmetic  6.18 us (1%)
    all_gather x1, waiting for transfers between devices, shards(): lax.all_gather(query_weight, 'req', axis=0, tiled=True)  135 us
    all_gather x1, waiting for transfers between devices, shards(): lax.all_gather(adapter_down, 'req', axis=0, tiled=True)  78 us
    all_gather x1, waiting for transfers between devices, shards(): lax.all_gather(keyvalue_weight, 'req', axis=0, tiled=True)  49.6 us
    all_gather x1, waiting for transfers between devices, shards(): normed = lax.all_gather(normed_part, 'blk', axis=1, tiled=True)  46.2 us
    all_gather x1, blocking collectives, shards(): lax.all_gather(adapter_up_keyvalue, 'req', axis=0, tiled=True)  40.4 us
    psum x1, blocking collectives, shards(): lax.psum(masked, 'blk').reshape(row_number, 3, rank_size)  26.5 us
    dot_general x2, matrix products, add_rows(): return jnp.dot(normed, weight_piece, preferred_element_type=jnp.float32)  18.4 us
    all_gather x1, waiting for transfers between devices, shards(): lax.all_gather(adapter_up_query, 'req', axis=0, tiled=True)  16 us
  transfers between devices with their start and end apart: 5, of which 5 were waited for; matrix products, arithmetic and copies ran while one was open for 5% of the time, Pallas kernels for 0%

commit v1 on v0

--- a/solution.py
+++ b/solution.py
@@ -62,7 +62,12 @@
     squares = lax.psum(jnp.sum(values * values, axis=1), "blk")
     factor = lax.rsqrt(squares / full_width + epsilon)
     normed_part = (values * factor[:, None] * gain_part[None, :]).astype(jnp.bfloat16)
-    normed = lax.all_gather(normed_part, "blk", axis=1, tiled=True)
+    ring = [normed_part]
+    for hop in range(7):
+        ring.append(lax.ppermute(ring[-1], "blk", [(dev, (dev + 1) % 8) for dev in range(8)]))
+    normed = jnp.roll(
+        jnp.concatenate(ring[::-1], axis=1), (lax.axis_index("blk") + 1) * ring[0].shape[1], axis=1
+    )
     query_cols = query_weight.shape[1]
 
     def add_rows(weight_piece):

time: 463 us -> 418 us (0.903)
  waiting for transfers between devices: 327 us -> 224 us
  starting transfers between devices: 0.19 us -> 23.1 us
  local copies, waits for them, and re-layouts: 2.7 us -> 23 us
  blocking collectives: 81.9 us -> 88.9 us
    all_gather x1, waiting for transfers between devices: 78 us -> 0.01 us  [shards(): lax.all_gather(adapter_down, 'req', axis=0, tiled=True)]
    ppermute x0 -> x7, waiting for transfers between devices: none -> 49.6 us  [shards(): lax.ppermute(ring[-1], 'blk', [(dev, (dev + 1) % 8) for dev in range(8)])]
    all_gather x1 -> x0, waiting for transfers between devices: 46.2 us -> none  [shards(): normed = lax.all_gather(normed_part, 'blk', axis=1, tiled=True)]
    ppermute x0 -> x7, starting transfers between devices: none -> 23 us  [shards(): lax.ppermute(ring[-1], 'blk', [(dev, (dev + 1) % 8) for dev in range(8)])]
    unnamed x20 -> x36, local copies, waits for them, and re-layouts: 1.8 us -> 22 us
    all_gather x1, waiting for transfers between devices: 16 us -> 0.01 us  [shards(): lax.all_gather(adapter_up_query, 'req', axis=0, tiled=True)]
    all_gather x1, waiting for transfers between devices: 49.6 us -> 36.9 us  [shards(): lax.all_gather(keyvalue_weight, 'req', axis=0, tiled=True)]
    psum x1, blocking collectives: 26.5 us -> 32.7 us  [shards(): lax.psum(masked, 'blk').reshape(row_number, 3, rank_size)]
  transfers between devices with their start and end apart: 5 -> 11, of which waited for: 5 -> 8; matrix products, arithmetic and copies ran while one was open for 5% -> 12% of each run, Pallas kernels for 0% -> 0%
where the time goes in v1:
time: 418 us; the launch traced here: 417 us
  waiting for transfers between devices  224 us (54%)
  blocking collectives  88.9 us (21%)
  matrix products  33.5 us (8%)
  starting transfers between devices  23.1 us (6%)
  local copies, waits for them, and re-layouts  23 us (6%)
  between operations  14 us (3%)
  other arithmetic  10.6 us (3%)
    all_gather x1, waiting for transfers between devices, shards(): lax.all_gather(query_weight, 'req', axis=0, tiled=True)  135 us
    ppermute x7, waiting for transfers between devices, shards(): lax.ppermute(ring[-1], 'blk', [(dev, (dev + 1) % 8) for dev in range(8)])  49.6 us
    all_gather x1, blocking collectives, shards(): lax.all_gather(adapter_up_keyvalue, 'req', axis=0, tiled=True)  41.2 us
    all_gather x1, waiting for transfers between devices, shards(): lax.all_gather(keyvalue_weight, 'req', axis=0, tiled=True)  36.9 us
    psum x1, blocking collectives, shards(): lax.psum(masked, 'blk').reshape(row_number, 3, rank_size)  32.7 us
    ppermute x7, starting transfers between devices, shards(): lax.ppermute(ring[-1], 'blk', [(dev, (dev + 1) % 8) for dev in range(8)])  23 us
    unnamed x36, local copies, waits for them, and re-layouts  22 us
    dot_general x2, matrix products, add_rows(): return jnp.dot(normed, weight_piece, preferred_element_type=jnp.float32)  18.7 us
  transfers between devices with their start and end apart: 11, of which 8 were waited for; matrix products, arithmetic and copies ran while one was open for 12% of the time, Pallas kernels for 0%

profile of v1, /device:TPU:1, one launch (start us, length us, event | category | flops | bytes accessed | tf_op | source)
XLA Modules:
  0.0 417.5 jit_solution(2999303451051125429)
XLA Ops:
  12.0 15.0 %psum.14 = f32[384]{0:T(512)S(1)} all-reduce(f32[384]{0:T(512)S(1)} %fusion.11), channel_id=1, replica_groups=mesh['blk'=8,'req'=32] {'blk'}, use_global_device_ids=true, to_apply=%region_1.0 | all-reduce | flops 384 | bytes 3072 | tf_op jit(solution)/shard_map/psum | solution.py:62
  28.5 8.9 %collective-permute-done = bf16[384,1024]{1,0:T(8,128)(2,1)S(1)} collective-permute-done((bf16[384,1024]{1,0:T(8,128)(2,1)S(1)}, bf16[384,1024]{1,0:T(8,128)(2,1)S(1)}, u32[]{:S(2)}, u32[]{:S(2)}) %collective-permute-start) | collective-permute-done | bytes 786464 | tf_op jit(solution)/shard_map/ppermute | solution.py:67
  37.4 2.5 collective-permute-start.1
  39.9 8.9 %collective-permute-done.1 = bf16[384,1024]{1,0:T(8,128)(2,1)S(1)} collective-permute-done((bf16[384,1024]{1,0:T(8,128)(2,1)S(1)}, bf16[384,1024]{1,0:T(8,128)(2,1)S(1)}, u32[]{:S(2)}, u32[]{:S(2)}) %collective-permute-start.1) | collective-permute-done | bytes 786464 | tf_op jit(solution)/shard_map/ppermute | solution.py:67
  48.8 2.5 collective-permute-start.2
  51.3 8.9 %collective-permute-done.2 = bf16[384,1024]{1,0:T(8,128)(2,1)S(1)} collective-permute-done((bf16[384,1024]{1,0:T(8,128)(2,1)S(1)}, bf16[384,1024]{1,0:T(8,128)(2,1)S(1)}, u32[]{:S(2)}, u32[]{:S(2)}) %collective-permute-start.2) | collective-permute-done | bytes 786464 | tf_op jit(solution)/shard_map/ppermute | solution.py:67
  60.2 2.5 collective-permute-start.3
  62.7 8.9 %collective-permute-done.3 = bf16[384,1024]{1,0:T(8,128)(2,1)S(1)} collective-permute-done((bf16[384,1024]{1,0:T(8,128)(2,1)S(1)}, bf16[384,1024]{1,0:T(8,128)(2,1)S(1)}, u32[]{:S(2)}, u32[]{:S(2)}) %collective-permute-start.3) | collective-permute-done | bytes 786464 | tf_op jit(solution)/shard_map/ppermute | solution.py:67
  71.7 2.5 collective-permute-start.4
  75.0 41.2 %all_gather.17 = bf16[32,16,256]{2,1,0:T(8,128)(2,1)S(1)} all-gather(bf16[1,16,256]{2,1,0:T(8,128)(2,1)} %param.15), channel_id=1, replica_groups=mesh['blk'=8,'req'=32] {'req'}, dimensions={0}, use_global_device_ids=true | all-gather | bytes 270336 | tf_op jit(solution)/shard_map/all_gather | solution.py:81
  117.0 10.6 %collective-permute-start.5 = (bf16[384,1024]{1,0:T(8,128)(2,1)}, bf16[384,1024]{1,0:T(8,128)(2,1)}, u32[]{:S(2)}, u32[]{:S(2)}) collective-permute-start(bf16[384,1024]{1,0:T(8,128)(2,1)} %collective-permute-done.4), channel_id=1, source_target_pairs={{0,32},{32,64},{64,96},{96,128},{128,160},{160,192},{192,224},{224... | collective-permute-start | bytes 2359304 | tf_op jit(solution)/shard_map/ppermute | solution.py:67
  128.5 8.3 %collective-permute-done.5 = bf16[384,1024]{1,0:T(8,128)(2,1)} collective-permute-done((bf16[384,1024]{1,0:T(8,128)(2,1)}, bf16[384,1024]{1,0:T(8,128)(2,1)}, u32[]{:S(2)}, u32[]{:S(2)}) %collective-permute-start.5) | collective-permute-done | bytes 786464 | tf_op jit(solution)/shard_map/ppermute | solution.py:67
  136.9 2.5 collective-permute-start.6
  140.9 3.1 convolution_convert_fusion
  144.0 5.5 %collective-permute-done.6 = bf16[384,1024]{1,0:T(8,128)(2,1)} collective-permute-done((bf16[384,1024]{1,0:T(8,128)(2,1)}, bf16[384,1024]{1,0:T(8,128)(2,1)}, u32[]{:S(2)}, u32[]{:S(2)}) %collective-permute-start.6) | collective-permute-done | bytes 786464 | tf_op jit(solution)/shard_map/ppermute | solution.py:67
  151.6 2.2 constant_dynamic-update-slice_fusion.14
  153.8 2.1 constant_dynamic-update-slice_fusion.13
  165.0 2.1 constant_dynamic-update-slice_fusion.5
  172.1 5.4 %fusion.21 = bf16[4,3,16,1024]{3,0,2,1:T(4,128)(2,1)S(1)} fusion(bf16[32,3,16,1024]{3,2,1,0:T(8,128)(2,1)} %all-gather.7.cloned.1.call-done, s32[4]{0:T(128)S(1)} %bitcast.135), kind=kOutput, calls=%fused_computation.27 | convolution fusion | flops 12779648 | bytes 3538960 | tf_op jit(solution)/shard_map/pa,ajrd->pjrd/dot_general | solution.py:90
  177.9 32.7 %psum.15 = bf16[384,48]{0,1:T(8,128)(2,1)S(1)} all-reduce(f32[384,48]{0,1:T(8,128)S(1)} %bitcast.130), channel_id=1, replica_groups=mesh['blk'=8,'req'=32] {'blk'}, use_global_device_ids=true, to_apply=%region_4.5 | all-reduce | flops 18432 | bytes 110592 | tf_op jit(solution)/shard_map/psum | solution.py:104
  212.2 36.9 %all-gather.5.cloned.1.call-done = bf16[8192,256]{1,0:T(8,128)(2,1)} async-done(((bf16[256,256]{1,0:T(8,128)(2,1)}), bf16[8192,256]{1,0:T(8,128)(2,1)}) %all-gather.5.cloned.1.call-update) | async-done | bytes 4194320 | tf_op jit(solution)/shard_map/all_gather | solution.py:77
  249.2 6.4 %fusion.2 = f32[384,256]{0,1:T(8,128)S(1)} fusion(bf16[8192,256]{1,0:T(8,128)(2,1)} %all-gather.5.cloned.1.call-done, bf16[384,16384]{1,0:T(8,128)(2,1)} %constant_dynamic-update-slice_fusion, s32[]{:T(128)S(6)} %select_n.26), kind=kOutput, calls=%fused_computation.2 | convolution fusion | flops 1610612736 | bytes 10878980 | tf_op jit(solution)/shard_map/dot_general | solution.py:74
  256.7 135.1 %all-gather.9.cloned.1.call-done = bf16[8192,1024]{1,0:T(8,128)(2,1)} async-done(((bf16[256,1024]{1,0:T(8,128)(2,1)}), bf16[8192,1024]{1,0:T(8,128)(2,1)}) %all-gather.9.cloned.1.call-update) | async-done | bytes 16777232 | tf_op jit(solution)/shard_map/all_gather | solution.py:76
  391.8 12.4 %fusion.15 = f32[384,1024]{1,0:T(8,128)S(1)} fusion(f32[384,1024,1]{1,0,2:T(8,128)} %fusion.40, bf16[8192,1024]{1,0:T(8,128)(2,1)} %all-gather.9.cloned.1.call-done, bf16[384,16384]{1,0:T(8,128)(2,1)} %constant_dynamic-update-slice_fusion, s32[]{:T(128)S(6)} %select_n.26), kind=kOutput, calls=%fused_computation.25 | convolution fusion | flops 6443237376 | bytes 26214404 | tf_op jit(solution)/shard_map/dot_general | solution.py:74
  (78 shorter events, 36.3 us)
Async XLA Ops:
  7.2 133.8 %all-gather.11.cloned.1.call-start = ((), (), s32[]{:S(2)}) async-start(), calls=%async_computation.3 | async-start | bytes 1081344 | tf_op jit(solution)/shard_map/all_gather | solution.py:80
  7.9 164.2 %all-gather.7.cloned.1.call-start = ((), (), s32[]{:S(2)}) async-start(), calls=%async_computation.1 | async-start | bytes 3244032 | tf_op jit(solution)/shard_map/all_gather | solution.py:79
  8.6 240.5 %all-gather.5.cloned.1.call-start = ((), (), s32[]{:S(2)}) async-start(), calls=%async_computation | async-start | bytes 4325376 | tf_op jit(solution)/shard_map/all_gather | solution.py:77
  9.4 382.5 %all-gather.9.cloned.1.call-start = ((), (), s32[]{:S(2)}) async-start(), calls=%async_computation.2 | async-start | bytes 17301504 | tf_op jit(solution)/shard_map/all_gather | solution.py:76
  28.4 43.2 %copy-start.1 = (bf16[384,1024]{1,0:T(8,128)(2,1)}, bf16[384,1024]{1,0:T(8,128)(2,1)S(1)}, u32[]{:S(2)}) copy-start(bf16[384,1024]{1,0:T(8,128)(2,1)S(1)} %fusion.13) | copy-start | bytes 2359300
  28.4 9.0 %collective-permute-start = (bf16[384,1024]{1,0:T(8,128)(2,1)S(1)}, bf16[384,1024]{1,0:T(8,128)(2,1)S(1)}, u32[]{:S(2)}, u32[]{:S(2)}) collective-permute-start(bf16[384,1024]{1,0:T(8,128)(2,1)S(1)} %fusion.13), channel_id=1, source_target_pairs={{0,32},{32,64},{64,96},{96,128},{128,160},{160,192},{192,224},{224... | collective-permute-start | bytes 2359304 | tf_op jit(solution)/shard_map/ppermute | solution.py:67
  37.4 11.4 %collective-permute-start.1 = (bf16[384,1024]{1,0:T(8,128)(2,1)S(1)}, bf16[384,1024]{1,0:T(8,128)(2,1)S(1)}, u32[]{:S(2)}, u32[]{:S(2)}) collective-permute-start(bf16[384,1024]{1,0:T(8,128)(2,1)S(1)} %collective-permute-done), channel_id=1, source_target_pairs={{0,32},{32,64},{64,96},{96,128},{128,160},{160,192},{192,224},{224... | collective-permute-start | bytes 2359304 | tf_op jit(solution)/shard_map/ppermute | solution.py:67
  48.8 11.4 %collective-permute-start.2 = (bf16[384,1024]{1,0:T(8,128)(2,1)S(1)}, bf16[384,1024]{1,0:T(8,128)(2,1)S(1)}, u32[]{:S(2)}, u32[]{:S(2)}) collective-permute-start(bf16[384,1024]{1,0:T(8,128)(2,1)S(1)} %collective-permute-done.1), channel_id=1, source_target_pairs={{0,32},{32,64},{64,96},{96,128},{128,160},{160,192},{192,224},{224... | collective-permute-start | bytes 2359304 | tf_op jit(solution)/shard_map/ppermute | solution.py:67
  60.2 11.4 %collective-permute-start.3 = (bf16[384,1024]{1,0:T(8,128)(2,1)S(1)}, bf16[384,1024]{1,0:T(8,128)(2,1)S(1)}, u32[]{:S(2)}, u32[]{:S(2)}) collective-permute-start(bf16[384,1024]{1,0:T(8,128)(2,1)S(1)} %collective-permute-done.2), channel_id=1, source_target_pairs={{0,32},{32,64},{64,96},{96,128},{128,160},{160,192},{192,224},{224... | collective-permute-start | bytes 2359304 | tf_op jit(solution)/shard_map/ppermute | solution.py:67
  71.7 45.4 %collective-permute-start.4 = (bf16[384,1024]{1,0:T(8,128)(2,1)S(1)}, bf16[384,1024]{1,0:T(8,128)(2,1)}, u32[]{:S(2)}, u32[]{:S(2)}) collective-permute-start(bf16[384,1024]{1,0:T(8,128)(2,1)S(1)} %collective-permute-done.3), channel_id=1, source_target_pairs={{0,32},{32,64},{64,96},{96,128},{128,160},{160,192},{192,224},{224... | collective-permute-start | bytes 2359304 | tf_op jit(solution)/shard_map/ppermute | solution.py:67
  117.0 19.8 %collective-permute-start.5 = (bf16[384,1024]{1,0:T(8,128)(2,1)}, bf16[384,1024]{1,0:T(8,128)(2,1)}, u32[]{:S(2)}, u32[]{:S(2)}) collective-permute-start(bf16[384,1024]{1,0:T(8,128)(2,1)} %collective-permute-done.4), channel_id=1, source_target_pairs={{0,32},{32,64},{64,96},{96,128},{128,160},{160,192},{192,224},{224... | collective-permute-start | bytes 2359304 | tf_op jit(solution)/shard_map/ppermute | solution.py:67
  136.9 12.6 %collective-permute-start.6 = (bf16[384,1024]{1,0:T(8,128)(2,1)}, bf16[384,1024]{1,0:T(8,128)(2,1)}, u32[]{:S(2)}, u32[]{:S(2)}) collective-permute-start(bf16[384,1024]{1,0:T(8,128)(2,1)} %collective-permute-done.5), channel_id=1, source_target_pairs={{0,32},{32,64},{64,96},{96,128},{128,160},{160,192},{192,224},{224... | collective-permute-start | bytes 2359304 | tf_op jit(solution)/shard_map/ppermute | solution.py:67
  151.6 8.1 %copy-start = (bf16[384,1024]{1,0:T(8,128)(2,1)S(1)}, bf16[384,1024]{1,0:T(8,128)(2,1)}, u32[]{:S(2)}) copy-start(bf16[384,1024]{1,0:T(8,128)(2,1)} %param.9) | copy-start | bytes 2359300
  165.0 7.0 %copy-start.7 = (s32[1,4]{1,0:T(1,128)S(1)}, s32[1,4]{1,0:T(1,128)}, u32[]{:S(2)}) copy-start(s32[1,4]{1,0:T(1,128)} %param.17) | copy-start | bytes 52
  168.1 9.4 %copy-start.2 = (bf16[384,1024]{1,0:T(8,128)(2,1)S(1)}, bf16[384,1024]{1,0:T(8,128)(2,1)}, u32[]{:S(2)}) copy-start(bf16[384,1024]{1,0:T(8,128)(2,1)} %copy-done.1) | copy-start | bytes 2359300
  170.0 40.7 %copy-start.5 = (bf16[4,16,1024]{2,0,1:T(4,128)(2,1)S(1)}, bf16[4,16,1024]{2,0,1:T(4,128)(2,1)}, u32[]{:S(2)}) copy-start(bf16[4,16,1024]{2,0,1:T(4,128)(2,1)} %convolution_convert_fusion) | copy-start | bytes 393220
  212.2 44.2 %copy-start.3 = (f32[384,64]{1,0:T(8,128)S(1)}, f32[384,64]{1,0:T(8,128)}, u32[]{:S(2)}) copy-start(f32[384,64]{1,0:T(8,128)} %get-tuple-element.31) | copy-start | bytes 294916
  256.1 152.0 %copy-start.6 = (bf16[384,128]{1,0:T(8,128)(2,1)}, bf16[384,128]{1,0:T(8,128)(2,1)S(1)}, u32[]{:S(2)}) copy-start(bf16[384,128]{1,0:T(8,128)(2,1)S(1)} %fusion.27) | copy-start | bytes 294916
  256.7 149.0 %copy-start.4 = (bf16[384,128]{1,0:T(8,128)(2,1)}, bf16[384,128]{1,0:T(8,128)(2,1)S(1)}, u32[]{:S(2)}) copy-start(bf16[384,128]{1,0:T(8,128)(2,1)S(1)} %get-tuple-element.18) | copy-start | bytes 294916
Sparse Core Ops, SparseCore 0:
  10.6 75.9 all-gather.10
  89.2 78.3 all-gather.6
  170.2 78.9 all-gather.4
  251.6 140.1 all-gather.8
